TPU v7x, 128 devices: a whole 4x4x4 slice. The times are simulated.
128 devices in a mesh: row: 8 (over x, z_hi), col: 4 (over y), rep: 4 (over z_lo, core).
Axes of the slice: x: 4, y: 4, z: 4 (z_hi: 2, z_lo: 2; z = z_hi * 2 + z_lo), core: 2. Of those that a mesh axis runs over, the one named last changes fastest.
Arguments:
- features: bfloat16 [65536, 256], P(('row', 'col', 'rep')), may hold values from -6 to 6
- blocks: bfloat16 [512, 128, 128, 128], P('row', ('col', 'rep')), may hold values from 0 to 0.015625
- block_cols: int32 [512, 128], P('row', ('col', 'rep')), may hold values from 0 to 31
- counts: int32 [512, 16], P('row', ('col', 'rep')), may hold values from 0 to 8, as said below
- weight: bfloat16 [256, 256], replicated, may hold values from -12 to 12
- bias: float32 [256], replicated, may hold values from -3 to 3
Outputs:
- hidden_out: bfloat16 [65536, 256], P(('row', 'col', 'rep'))
Inputs may be any that keep to these rules, and one draw needn't show every extreme that they name: A block row's live slots in a column shard are its first counts slots.
All inputs are finite; a program needn't handle non-finite values.
Results may differ from a plain program's by a relative error of at most 0.02.
Values may be sent and summed in bfloat16 or wider, within the bound.
A program may use at most 192 MiB of HBM per device.

v0:
```python
import jax
import jax.numpy as jnp
from jax import lax
from jax.sharding import PartitionSpec as P


def shards(features, blocks, block_cols, counts, weight, bias):
    block_rows, slot_count, block_size, _ = blocks.shape
    row_count, feature_width = features.shape
    count_column = counts[:, 0]
    slot_ids = lax.broadcasted_iota(jnp.int32, (block_rows, slot_count), 1)
    live_slots = slot_ids < count_column[:, None]
    block_sums = jnp.sum(blocks, axis=3, dtype=jnp.float32)
    row_part = jnp.sum(jnp.where(live_slots[:, :, None], block_sums, 0.0), axis=1).reshape(
        block_rows * block_size
    )
    own_sums = lax.psum_scatter(
        row_part.astype(jnp.bfloat16), ("col", "rep"), scatter_dimension=0, tiled=True
    ).astype(jnp.float32)
    inverse_root = lax.rsqrt(1.0 + own_sums)
    scaled = (inverse_root[:, None] * features.astype(jnp.float32)).astype(jnp.bfloat16)
    gathered = lax.all_gather(scaled, "row", axis=0, tiled=True)
    panel_blocks = gathered.reshape(gathered.shape[0] // block_size, block_size, feature_width)
    count = row_count * lax.axis_size(("col", "rep"))
    block_count = count // block_size
    running = jnp.zeros((block_count, block_size, feature_width), jnp.float32)
    for slot_number in range(slot_count):
        tile_values = lax.dynamic_index_in_dim(blocks, slot_number, 1, keepdims=False)
        column_index = lax.dynamic_index_in_dim(block_cols, slot_number, 1, keepdims=False)
        slot_alive = lax.dynamic_index_in_dim(live_slots, slot_number, 1, keepdims=False)
        picked = jnp.take(panel_blocks, column_index, axis=0)
        product = jnp.einsum(
            "iab,ibf->iaf", tile_values, picked, preferred_element_type=jnp.float32
        )
        running = running + jnp.where(slot_alive[:, None, None], product, 0.0)
    summed = lax.psum_scatter(
        running.reshape(count, feature_width).astype(jnp.bfloat16),
        ("col", "rep"),
        scatter_dimension=0,
        tiled=True,
    ).astype(jnp.float32)
    aggregated = (inverse_root[:, None] * (summed + scaled.astype(jnp.float32))).astype(
        jnp.bfloat16
    )
    mixed = jnp.dot(aggregated, weight, preferred_element_type=jnp.float32) + bias
    return jnp.maximum(mixed, 0.0).astype(jnp.bfloat16)


def solution(mesh):
    return jax.shard_map(
        shards,
        mesh=mesh,
        in_specs=(
            P(("row", "col", "rep"), None),
            P("row", ("col", "rep"), None, None),
            P("row", ("col", "rep")),
            P("row", ("col", "rep")),
            P(),
            P(),
        ),
        out_specs=P(("row", "col", "rep"), None),
        check_vma=False,
    )
```

profile of v0, /device:TPU:0, one launch (start us, length us, event | category | flops | bytes accessed | tf_op | source)
XLA Modules:
  0.0 293.6 jit_solution(11611073505402447153)
XLA Ops:
  6.5 0.0 copy-start
  6.5 0.0 all-gather.2.cloned.1.call-start
  6.5 0.7 iota_compare_fusion
  7.2 0.1 copy.25
  7.3 0.0 copy-start.11
  7.3 0.0 copy-start.8
  7.4 0.0 copy-start.9
  7.4 10.0 %convert_reduce_fusion = f32[64,8,128]{2,1,0:T(8,128)S(1)} fusion(bf16[64,8,128,128]{3,2,1,0:T(8,128)(2,1)} %param.9), kind=kLoop, calls=%fused_computation.8 | loop fusion | flops 16711680 | bytes 17039360 | tf_op jit(solution)/shard_map/reduce_sum | solution.py:13
  17.4 0.2 select_reduce_fusion
  17.6 56.7 %all-reduce = bf16[8192]{0:T(1024)(128)(2,1)S(1)} all-reduce(bf16[8192]{0:T(1024)(128)(2,1)S(1)} %bitcast.101), channel_id=2, replica_groups=mesh['row'=8,'col'=4,'rep'=4] {'col','rep'}, use_global_device_ids=true, to_apply=%region_2.3.clone | all-reduce | flops 8192 | bytes 32768
  74.2 0.0 copy-done.11
  74.2 0.6 dynamic-slice
  75.5 0.1 add_rsqrt_fusion
  75.5 0.0 copy-done.8
  75.5 0.8 multiply_convert_fusion.1
  76.4 0.0 all-gather.2.cloned.1.call-update
  76.4 0.0 reduce-scatter.2.cloned.1.call-start
  76.5 0.0 copy-done.9
  76.6 54.3 %all-gather.2.cloned.1.call-done = bf16[4096,256]{1,0:T(8,128)(2,1)} async-done(((bf16[512,256]{1,0:T(8,128)(2,1)}), bf16[4096,256]{1,0:T(8,128)(2,1)}) %all-gather.2.cloned.1.call-update) | async-done | bytes 2097168 | tf_op jit(solution)/shard_map/all_gather | solution.py:22
  130.8 0.0 copy-start.1
  130.8 4.5 %gather_fusion.2 = bf16[64,128,256]{2,1,0:T(8,128)(2,1)} fusion(bf16[32,128,256]{2,1,0:T(8,128)(2,1)} %bitcast.90, s32[1024]{0:T(1024)S(1)} %get-tuple-element.49), kind=kCustom, calls=%fused_computation.2.clone | custom fusion | bytes 8388864 | tf_op jit(solution)/shard_map/jit(_take)/gather | solution.py:31
  135.4 0.0 copy-done.1
  135.4 2.7 gather_fusion.1
  138.1 2.8 gather_fusion.6
  140.9 2.8 gather_fusion.5
  143.7 2.9 gather_fusion.4
  146.5 2.8 gather_fusion.3
  149.3 2.9 gather_fusion.7
  152.2 2.7 gather_fusion
  154.9 0.0 copy-start.7
  154.9 0.0 slice-start
  154.9 0.0 slice-start.1
  154.9 8.6 %fusion.10 = f32[64,256,128]{1,2,0:T(8,128)} fusion(bf16[64,128,256]{2,1,0:T(8,128)(2,1)} %gather_fusion.2, pred[64]{0:T(512)(128)(4,1)S(1)} %get-tuple-element.28, bf16[64,8,128,128]{3,2,1,0:T(8,128)(2,1)} %param.9), kind=kOutput, calls=%fused_computation.20 | convolution fusion | flops 538968064 | bytes 14680128 | tf_op jit(solution)/shard_map/iab,ibf->iaf/dot_general | solution.py:32
  163.5 0.0 copy-done.7
  163.5 0.0 copy-start.6
  163.5 0.0 slice-start.2
  163.5 6.3 %fusion.12 = f32[64,256,128]{1,2,0:T(8,128)} fusion(bf16[64,128,256]{2,1,0:T(8,128)(2,1)S(1)} %copy-done.7, pred[64]{0:T(512)(128)(4,1)S(1)} %get-tuple-element.30, bf16[64,8,128,128]{3,2,1,0:T(8,128)(2,1)} %param.9), kind=kOutput, calls=%fused_computation.22 | convolution fusion | flops 538968064 | bytes 14680128 | tf_op jit(solution)/shard_map/iab,ibf->iaf/dot_general | solution.py:32
  169.8 0.0 copy-done.6
  169.8 0.0 slice-start.3
  169.9 0.0 copy-start.2
  169.9 6.3 %fusion.2 = f32[64,256,128]{1,2,0:T(8,128)} fusion(bf16[64,128,256]{2,1,0:T(8,128)(2,1)S(1)} %copy-done.6, pred[64]{0:T(512)(128)(4,1)S(1)} %get-tuple-element.34, bf16[64,8,128,128]{3,2,1,0:T(8,128)(2,1)} %param.9), kind=kOutput, calls=%fused_computation.12 | convolution fusion | flops 538968064 | bytes 14680128 | tf_op jit(solution)/shard_map/iab,ibf->iaf/dot_general | solution.py:32
  176.2 0.0 slice-done
  176.2 0.0 slice-done.1
  176.2 0.0 slice-done.2
  176.2 0.0 slice-done.3
  176.2 0.0 copy-done.2
  176.2 0.0 copy-start.3
  176.2 4.6 %fusion.4 = f32[64,256,128]{1,2,0:T(8,128)} fusion(bf16[64,128,256]{2,1,0:T(8,128)(2,1)S(1)} %copy-done.2, pred[64]{0:T(512)(128)(4,1)S(1)} %get-tuple-element.22, bf16[64,8,128,128]{3,2,1,0:T(8,128)(2,1)S(1)} %bitcast.99), kind=kOutput, calls=%fused_computation.14 | convolution fusion | flops 538968064 | bytes 14680576 | tf_op jit(solution)/shard_map/iab,ibf->iaf/dot_general | solution.py:32
  180.8 0.0 copy-done.3
  180.8 0.0 copy-start.4
  180.8 4.6 %fusion.6 = f32[64,256,128]{1,2,0:T(8,128)} fusion(bf16[64,128,256]{2,1,0:T(8,128)(2,1)S(1)} %copy-done.3, pred[64]{0:T(512)(128)(4,1)S(1)} %get-tuple-element.24, bf16[64,8,128,128]{3,2,1,0:T(8,128)(2,1)S(1)} %bitcast.99), kind=kOutput, calls=%fused_computation.16 | convolution fusion | flops 538968064 | bytes 14680576 | tf_op jit(solution)/shard_map/iab,ibf->iaf/dot_general | solution.py:32
  185.4 0.0 copy-done.4
  185.4 0.0 copy-start.5
  185.4 4.5 %fusion.8 = f32[64,256,128]{1,2,0:T(8,128)} fusion(bf16[64,128,256]{2,1,0:T(8,128)(2,1)S(1)} %copy-done.4, pred[64]{0:T(512)(128)(4,1)S(1)} %get-tuple-element.26, bf16[64,8,128,128]{3,2,1,0:T(8,128)(2,1)S(1)} %bitcast.99), kind=kOutput, calls=%fused_computation.18 | convolution fusion | flops 538968064 | bytes 14680576 | tf_op jit(solution)/shard_map/iab,ibf->iaf/dot_general | solution.py:32
  189.9 0.0 copy-done.5
  189.9 4.6 %fusion = f32[64,256,128]{1,2,0:T(8,128)} fusion(bf16[64,128,256]{2,1,0:T(8,128)(2,1)S(1)} %copy-done.5, pred[64]{0:T(512)(128)(4,1)S(1)} %get-tuple-element.32, bf16[64,8,128,128]{3,2,1,0:T(8,128)(2,1)S(1)} %bitcast.99), kind=kOutput, calls=%fused_computation.10 | convolution fusion | flops 538968064 | bytes 14680576 | tf_op jit(solution)/shard_map/iab,ibf->iaf/dot_general | solution.py:32
  194.5 23.9 %add_convert_fusion = bf16[64,256,128]{1,2,0:T(8,128)(2,1)} fusion(f32[64,256,128]{1,2,0:T(8,128)} %fusion, f32[64,256,128]{1,2,0:T(8,128)} %fusion.2, f32[64,256,128]{1,2,0:T(8,128)} %fusion.4, f32[64,256,128]{1,2,0:T(8,128)} %fusion.6, f32[64,256,128]{1,2,0:T(8,128)} %fusion.8, f32[64,256,128]{1,2,0:T(8,128)} %fusion.10, f32[64,256,128]{1,2,0:T(8,128)} %fusion.12, ...), kind=kOutput, calls=%fused_computation.9 | convolution fusion | flops 572522496 | bytes 69206592 | tf_op jit(solution)/shard_map/iab,ibf->iaf/dot_general | solution.py:32
  218.4 0.0 copy-start.10
  218.4 0.0 reduce-scatter.2.cloned.1.call-update
  218.4 66.4 %reduce-scatter.2.cloned.1.call-done = bf16[512,256]{1,0:T(8,128)(2,1)} async-done(((bf16[8192,256]{1,0:T(8,128)(2,1)}), bf16[512,256]{1,0:T(8,128)(2,1)}) %reduce-scatter.2.cloned.1.call-update) | async-done | bytes 262160 | tf_op jit(solution)/shard_map/reduce_scatter | solution.py:36
  284.8 0.0 copy-done
  284.8 0.0 copy-done.10
  284.8 2.0 fusion.51
  (7 shorter events, 0.1 us)
Async XLA Ops:
  6.5 278.3 %copy-start = (bf16[256,256]{1,0:T(8,128)(2,1)S(1)}, bf16[256,256]{1,0:T(8,128)(2,1)}, u32[]{:S(2)}) copy-start(bf16[256,256]{1,0:T(8,128)(2,1)} %param.12) | copy-start | bytes 393220
  6.5 124.3 %all-gather.2.cloned.1.call-start = ((), (), s32[]{:S(2)}) async-start(), calls=%async_computation.1 | async-start | bytes 2359296 | tf_op jit(solution)/shard_map/all_gather | solution.py:22
  7.3 66.9 %copy-start.11 = (u32[128]{0:T(128)S(1)}, u32[128]{0:T(128)}, u32[]{:S(2)}) copy-start(u32[128]{0:T(128)} %constant.90) | copy-start | bytes 1540
  7.3 68.2 %copy-start.8 = (bf16[512,256]{1,0:T(8,128)(2,1)S(1)}, bf16[512,256]{1,0:T(8,128)(2,1)}, u32[]{:S(2)}) copy-start(bf16[512,256]{1,0:T(8,128)(2,1)} %param.8) | copy-start | bytes 786436
  7.4 69.1 %copy-start.9 = (s32[64,8]{0,1:T(8,128)S(1)}, s32[64,8]{0,1:T(8,128)}, u32[]{:S(2)}) copy-start(s32[64,8]{0,1:T(8,128)} %param.10) | copy-start | bytes 6148
  76.4 208.4 %reduce-scatter.2.cloned.1.call-start = ((), (), s32[]{:S(2)}) async-start(), calls=%async_computation.2 | async-start | bytes 4456448 | tf_op jit(solution)/shard_map/reduce_scatter | solution.py:36
  130.8 4.5 %copy-start.1 = (bf16[4096,256]{1,0:T(8,128)(2,1)S(1)}, bf16[4096,256]{1,0:T(8,128)(2,1)}, u32[]{:S(2)}) copy-start(bf16[4096,256]{1,0:T(8,128)(2,1)} %all-gather.2.cloned.1.call-done) | copy-start | bytes 6291460
  154.9 8.6 %copy-start.7 = (bf16[64,128,256]{2,1,0:T(8,128)(2,1)S(1)}, bf16[64,128,256]{2,1,0:T(8,128)(2,1)}, u32[]{:S(2)}) copy-start(bf16[64,128,256]{2,1,0:T(8,128)(2,1)} %gather_fusion.1) | copy-start | bytes 12582916
  154.9 21.3 %slice-start = ((s8[16777216]{0:T(1024)(128)(4,1)}), s8[4194304]{0:T(1024)(128)(4,1)S(1)}, s32[]{:S(2)}) async-start(s8[16777216]{0:T(1024)(128)(4,1)} %bitcast.98), calls=%async_computation.3 | async-start | bytes 8388608
  154.9 21.3 %slice-start.1 = ((s8[16777216]{0:T(1024)(128)(4,1)}), s8[4194304]{0:T(1024)(128)(4,1)S(1)}, s32[]{:S(2)}) async-start(s8[16777216]{0:T(1024)(128)(4,1)} %bitcast.98), calls=%async_computation.4 | async-start | bytes 8388608
  163.5 6.3 %copy-start.6 = (bf16[64,128,256]{2,1,0:T(8,128)(2,1)S(1)}, bf16[64,128,256]{2,1,0:T(8,128)(2,1)}, u32[]{:S(2)}) copy-start(bf16[64,128,256]{2,1,0:T(8,128)(2,1)} %gather_fusion.6) | copy-start | bytes 12582916
  163.5 12.7 %slice-start.2 = ((s8[16777216]{0:T(1024)(128)(4,1)}), s8[4194304]{0:T(1024)(128)(4,1)S(1)}, s32[]{:S(2)}) async-start(s8[16777216]{0:T(1024)(128)(4,1)} %bitcast.98), calls=%async_computation.5 | async-start | bytes 8388608
  169.8 6.4 %slice-start.3 = ((s8[16777216]{0:T(1024)(128)(4,1)}), s8[4194304]{0:T(1024)(128)(4,1)S(1)}, s32[]{:S(2)}) async-start(s8[16777216]{0:T(1024)(128)(4,1)} %bitcast.98), calls=%async_computation.6 | async-start | bytes 8388608
  169.9 6.4 %copy-start.2 = (bf16[64,128,256]{2,1,0:T(8,128)(2,1)S(1)}, bf16[64,128,256]{2,1,0:T(8,128)(2,1)}, u32[]{:S(2)}) copy-start(bf16[64,128,256]{2,1,0:T(8,128)(2,1)} %gather_fusion.5) | copy-start | bytes 12582916
  176.2 4.6 %copy-start.3 = (bf16[64,128,256]{2,1,0:T(8,128)(2,1)S(1)}, bf16[64,128,256]{2,1,0:T(8,128)(2,1)}, u32[]{:S(2)}) copy-start(bf16[64,128,256]{2,1,0:T(8,128)(2,1)} %gather_fusion.4) | copy-start | bytes 12582916
  180.8 4.6 %copy-start.4 = (bf16[64,128,256]{2,1,0:T(8,128)(2,1)S(1)}, bf16[64,128,256]{2,1,0:T(8,128)(2,1)}, u32[]{:S(2)}) copy-start(bf16[64,128,256]{2,1,0:T(8,128)(2,1)} %gather_fusion.3) | copy-start | bytes 12582916
  185.4 4.5 %copy-start.5 = (bf16[64,128,256]{2,1,0:T(8,128)(2,1)S(1)}, bf16[64,128,256]{2,1,0:T(8,128)(2,1)}, u32[]{:S(2)}) copy-start(bf16[64,128,256]{2,1,0:T(8,128)(2,1)} %gather_fusion.7) | copy-start | bytes 12582916
  218.4 66.4 %copy-start.10 = (f32[256]{0:T(256)S(1)}, f32[256]{0:T(256)}, u32[]{:S(2)}) copy-start(f32[256]{0:T(256)} %param.13) | copy-start | bytes 3076
Sparse Core Ops, SparseCore 0:
  76.5 54.2 all-gather.1
  218.5 66.2 reduce-scatter.1
where the time goes:
time: 294 us
  waiting for transfers between devices  121 us (41%)
  matrix products  65.3 us (22%)
  blocking collectives  56.7 us (19%)
  local copies, waits for them, and re-layouts  24.9 us (8%)
  between operations  14.2 us (5%)
  other arithmetic  11.8 us (4%)
    reduce_scatter x1, waiting for transfers between devices, shards(): lax.psum_scatter(running.reshape(count, feature_width).astype(jnp.bfloat1...  66.4 us
    dot_general x8, matrix products, shards(): jnp.einsum('iab,ibf->iaf', tile_values, picked, preferred_element_type=jn...  63.4 us
    unnamed x1, blocking collectives  56.7 us
    all_gather x1, waiting for transfers between devices, shards(): gathered = lax.all_gather(scaled, 'row', axis=0, tiled=True)  54.3 us
    gather x8, local copies, waits for them, and re-layouts, shards(): picked = jnp.take(panel_blocks, column_index, axis=0)  24.1 us
    reduce_sum x1, other arithmetic, shards(): block_sums = jnp.sum(blocks, axis=3, dtype=jnp.float32)  10 us
  transfers between devices with their start and end apart: 2, of which 2 were waited for; matrix products, arithmetic and copies ran while one was open for 0% of the time, Pallas kernels for 0%

commit v1 on v0

v1 whole, which is shorter than its diff:
```python
import functools

import jax
import jax.numpy as jnp
from jax import lax
from jax.experimental import pallas as pl
from jax.experimental.pallas import tpu as pltpu
from jax.sharding import PartitionSpec as P

MESH = pl.DeviceIdType.MESH
BF16, F32 = jnp.bfloat16, jnp.float32
HALVES = 2
PRE = 6
MIDDLE = 12
GATHER_Z = 512
REDUCE_Z = 0
LAG = 2
ORDER = ((2, 0), (2, 1), (1, 0), (3, 0), (1, 1), (3, 1), (0, 0), (0, 1))


def kernel(cnt, cols, feat, blocks, weight, bias, out, blk, raw, pan, inv_t, rs_tx, rs_rx, inv_tx, inv_rx, part, sib_rx, acc,
           ab_rx, p_rx, m_rx, z_rx, agg, bsem, fsem, ssem, rsem):
    row, col, rep = lax.axis_index("row"), lax.axis_index("col"), lax.axis_index("rep")
    x, zh, zl, c = row // 2, row % 2, rep // 2, rep % 2
    q = col * 4 + rep
    n_chunk = 16
    brows = blk.shape[0] // n_chunk
    width = raw.shape[-1]

    def row_peer(i):
        return (lax.rem(row + i, 8), col, rep)

    def col_peer(i):
        p = lax.rem(q + i, 16)
        return (row, p // 4, p % 4)

    sib = (row, col, zl * 2 + 1 - c)
    y_next, y_prev = (row, lax.rem(col + 1, 4), rep), (row, lax.rem(col + 3, 4), rep)
    z_near = (row, col, (1 - zl) * 2 + c)
    x_next, x_prev = (lax.rem(x + 1, 4) * 2 + zh, col, rep), (lax.rem(x + 3, 4) * 2 + zh, col, rep)
    z_far = (x * 2 + 1 - zh, col, rep)

    barrier = pltpu.get_barrier_semaphore()
    for i in range(1, 8):
        pl.semaphore_signal(barrier, inc=1, device_id=row_peer(i), device_id_type=MESH)
    for i in range(1, 16):
        pl.semaphore_signal(barrier, inc=1, device_id=col_peer(i), device_id_type=MESH)

    feat_copies = []
    for h in range(HALVES):
        copy = pltpu.make_async_copy(feat.at[:, pl.ds(h * width, width)], raw.at[h, row], fsem.at[h])
        copy.start()
        feat_copies.append(copy)
    block_copies = []
    for k in range(n_chunk):
        here = pl.ds(k * brows, brows)
        copy = pltpu.make_async_copy(blocks.at[here], blk.at[here], bsem.at[k])
        copy.start()
        block_copies.append(copy)

    numbers, pending = {}, []

    def number(name):
        return numbers.setdefault(name, len(numbers))

    def send(name, src, dst, device):
        m = number(name)
        copy = pltpu.make_async_remote_copy(
            src_ref=src, dst_ref=dst, send_sem=ssem.at[m], recv_sem=rsem.at[m], device_id=device, device_id_type=MESH
        )
        copy.start()
        pending.append(copy)

    def recv(name, place):
        m = number(name)
        pltpu.make_async_remote_copy(
            src_ref=place, dst_ref=place, send_sem=ssem.at[m], recv_sem=rsem.at[m], device_id=sib, device_id_type=MESH
        ).wait_recv()

    rs_tx[...] = jnp.zeros_like(rs_tx)
    for h in range(HALVES):
        pan[h, 32] = jnp.zeros((128, width), BF16)

    def row_sums(k):
        block_copies[k].wait()
        for j in range(brows):
            i = k * brows + j
            live = cnt[0, i]
            total = jnp.zeros((128, 128), F32)
            for s in range(8):
                total = total + jnp.where(s < live, blk[i, s].astype(F32), 0.0)
            rs_tx[k, j : j + 1, :] = jnp.sum(total.T, axis=0, keepdims=True)

    ga, gb = 256 - GATHER_Z // 2, 256 + GATHER_Z // 2
    g_mid, g_outer = pl.ds(ga, GATHER_Z), (pl.ds(0, ga), pl.ds(gb, 512 - gb))
    at_next, at_prev, at_two = lax.rem(x + 1, 4), lax.rem(x + 3, 4), lax.rem(x + 2, 4)
    low, high = pl.ds(0, 256), pl.ds(256, 256)

    def piece(h, xs, z, rows):
        return raw.at[h, xs * 2 + z, rows]

    def outward(h, what, xs, sides=(0, 1)):
        if GATHER_Z < 512:
            for side in sides:
                here = piece(h, xs, zh, g_outer[side])
                send(("gzo", h, what, side), here, here, z_far)

    def gather_0(h):
        feat_copies[h].wait()
        own = raw.at[h, row]
        mid = piece(h, x, zh, g_mid)
        send(("gx+", h), own, own, x_next)
        send(("gx-", h), own, own, x_prev)
        send(("gz", h), mid, mid, z_far)
        outward(h, 0, x)

    def gather_1(h):
        mid = piece(h, x, 1 - zh, g_mid)
        recv(("gz", h), mid)
        send(("gzx+", h), mid, mid, x_next)
        send(("gzx-", h), mid, mid, x_prev)
        recv(("gx+", h), raw.at[h, at_prev * 2 + zh])
        here = piece(h, at_prev, zh, low)
        send(("gxx+", h), here, here, x_next)
        recv(("gx-", h), raw.at[h, at_next * 2 + zh])
        here = piece(h, at_next, zh, high)
        send(("gxx-", h), here, here, x_prev)
        outward(h, 1, at_prev)
        outward(h, 2, at_next)

    def gather_2(h):
        recv(("gzx+", h), piece(h, at_prev, 1 - zh, g_mid))
        here = piece(h, at_prev, 1 - zh, pl.ds(ga, 256 - ga))
        send(("gzxx+", h), here, here, x_next)
        recv(("gzx-", h), piece(h, at_next, 1 - zh, g_mid))
        here = piece(h, at_next, 1 - zh, pl.ds(256, gb - 256))
        send(("gzxx-", h), here, here, x_prev)
        recv(("gxx+", h), piece(h, at_two, zh, low))
        outward(h, 3, at_two, (0,))
        recv(("gxx-", h), piece(h, at_two, zh, high))
        outward(h, 3, at_two, (1,))

    def gather_3(h):
        recv(("gzxx+", h), piece(h, at_two, 1 - zh, pl.ds(ga, 256 - ga)))
        recv(("gzxx-", h), piece(h, at_two, 1 - zh, pl.ds(256, gb - 256)))
        if GATHER_Z < 512:
            for what, xs in enumerate((x, at_prev, at_next, at_two)):
                for side in (0, 1):
                    recv(("gzo", h, what, side), piece(h, xs, 1 - zh, g_outer[side]))

    def scale(h):
        def group(r, _):
            for j in range(4):
                rows = pl.ds(j * 128, 128)
                factor = inv_t[r, :, j : j + 1]
                pan[h, r * 4 + j] = (raw[h, r, rows, :].astype(F32) * factor).astype(BF16)
            return 0

        lax.fori_loop(0, 8, group, 0, unroll=2)

    def product(h, slot, side, chip, core):
        first = (chip * 2 + core) * 4
        for j in range(4):
            i = first + j
            live = cnt[0, i]
            picked = jnp.concatenate([pan[h, jnp.where(s < live, cols[s, i], 32)] for s in range(8)], axis=0)
            tile = jnp.concatenate([blk[i, s] for s in range(8)], axis=1)
            part[h, slot, side, pl.ds(j * 128, 128), :] = jnp.dot(tile, picked, preferred_element_type=F32).astype(BF16)

    def unit(h, off, zc):
        slot = off * 2 + zc
        chip = lax.rem(col + off, 4) * 2 + (zl if zc else 1 - zl)
        product(h, slot, 0, chip, 1 - c)
        send(("sib", h, slot), part.at[h, slot, 0], sib_rx.at[h, slot], sib)
        product(h, slot, 1, chip, c)

    ra, rb = 256 - REDUCE_Z // 2, 256 + REDUCE_Z // 2
    ranges = [(lo, hi) for lo, hi in ((0, ra), (ra, 256), (256, rb), (rb, 512)) if hi > lo]

    def moved(name, h, off, zc, src, dst, device, lo, hi):
        if hi > lo:
            rows = pl.ds(lo, hi - lo)
            send((name, h, off, zc, lo), src.at[rows], dst.at[rows], device)

    def arrived(name, h, off, zc, dst, lo, hi):
        if hi > lo:
            recv((name, h, off, zc, lo), dst.at[pl.ds(lo, hi - lo)])

    def combine(h, off, zc):
        slot = off * 2 + zc
        last = zc == 1 and off == 0
        recv(("sib", h, slot), sib_rx.at[h, slot])
        cuts = ((0, 512),) if zc else ((0, ra), (rb, 512))
        if off == 1:
            arrived("ab+", h, 2, zc, ab_rx.at[h, zc], 0, 256 if zc else ra)
        if off == 3:
            arrived("ab-", h, 2, zc, ab_rx.at[h, zc], 256 if zc else rb, 512)
        if off == 0:
            for lo, hi in cuts:
                arrived("p", h, 1, zc, p_rx.at[h, zc], lo, hi)
                arrived("m", h, 3, zc, m_rx.at[h, zc], lo, hi)
        if zc == 1:
            arrived("zm", h, off, 0, z_rx.at[h, off], ra, rb)
            if off == 0:
                arrived("zo", h, off, 0, z_rx.at[h, off], 0, ra)
                arrived("zo", h, off, 0, z_rx.at[h, off], rb, 512)
        sums = []
        for lo, hi in ranges:
            rows = pl.ds(lo, hi - lo)
            mid = lo >= ra and hi <= rb
            total = part[h, slot, 1, rows, :].astype(F32) + sib_rx[h, slot, rows, :].astype(F32)
            if (off == 1 and hi <= 256 or off == 3 and lo >= 256) and (zc == 1 or not mid):
                total = total + ab_rx[h, zc, rows, :].astype(F32)
            if off == 0 and (zc == 1 or not mid):
                total = total + p_rx[h, zc, rows, :].astype(F32) + m_rx[h, zc, rows, :].astype(F32)
            if zc == 1 and (mid or off == 0):
                total = total + z_rx[h, off, rows, :].astype(F32)
            if last:
                sums.append(total)
            else:
                acc[h, slot, rows, :] = total.astype(BF16)
        if last:
            return jnp.concatenate(sums, axis=0)
        src = acc.at[h, slot]
        if zc == 0:
            moved("zm", h, off, zc, src, z_rx.at[h, off], z_near, ra, rb)
        if off == 2:
            moved("ab+", h, off, zc, src, ab_rx.at[h, zc], y_next, 0, 256 if zc else ra)
            moved("ab-", h, off, zc, src, ab_rx.at[h, zc], y_prev, 256 if zc else rb, 512)
        for lo, hi in cuts:
            if off == 1:
                moved("p", h, off, zc, src, p_rx.at[h, zc], y_next, lo, hi)
            if off == 3:
                moved("m", h, off, zc, src, m_rx.at[h, zc], y_prev, lo, hi)
            if off == 0:
                moved("zo", h, off, zc, src, z_rx.at[h, off], z_near, lo, hi)
        return None

    def finish(h, total):
        for j in range(4):
            rows = slice(j * 128, j * 128 + 128)
            factor = inv_t[8, :, j : j + 1]
            own = pan[h, row * 4 + j].astype(F32)
            agg[rows, h * width : (h + 1) * width] = (factor * (total[rows] + own)).astype(BF16)

    for k in range(PRE):
        row_sums(k)
    pl.semaphore_wait(barrier, 22)
    gather_0(0)
    for k in range(PRE, MIDDLE):
        row_sums(k)
    gather_1(0)
    gather_0(1)
    for k in range(MIDDLE, n_chunk):
        row_sums(k)
    for i in range(1, 16):
        to = lax.rem(q + i, 16)
        send(("rs", i), rs_tx.at[to], rs_rx.at[q], col_peer(i))
    rs_rx[q] = rs_tx[q]
    gather_2(0)
    for i in range(1, 16):
        recv(("rs", i), rs_rx.at[lax.rem(q + 16 - i, 16)])
    degree = rs_rx[0]
    for i in range(1, 16):
        degree = degree + rs_rx[i]
    inv_tx[...] = lax.rsqrt(1.0 + degree)
    for i in range(1, 8):
        send(("inv", i), inv_tx, inv_rx.at[row], row_peer(i))
    inv_rx[row] = inv_tx[...]
    gather_1(1)
    for i in range(1, 8):
        recv(("inv", i), inv_rx.at[lax.rem(row + 8 - i, 8)])
    for r in range(8):
        inv_t[r] = inv_rx[r].T
    inv_t[8] = inv_tx[...].T
    gather_3(0)
    scale(0)

    waiting = []
    for h in range(HALVES):
        if h == 1:
            gather_3(1)
            scale(1)
        for n, (off, zc) in enumerate(ORDER):
            unit(h, off, zc)
            waiting.append((h, off, zc))
            if h == 0 and n == 1:
                gather_2(1)
            if len(waiting) > LAG:
                h_, off_, zc_ = waiting.pop(0)
                total = combine(h_, off_, zc_)
                if total is not None:
                    finish(h_, total)
    for h_, off_, zc_ in waiting:
        total = combine(h_, off_, zc_)
        if total is not None:
            finish(h_, total)
    mixed = jnp.dot(agg[...], weight[...], preferred_element_type=F32) + bias[...]
    out[...] = jnp.maximum(mixed, 0.0).astype(BF16)
    for copy in pending:
        copy.wait_send()
    assert len(numbers) <= ssem.shape[0]


def shards(features, blocks, block_cols, counts, weight, bias):
    rows, width = features.shape
    half = width // HALVES
    vmem, smem, anywhere = (pl.BlockSpec(memory_space=s) for s in (pltpu.VMEM, pltpu.SMEM, pl.ANY))
    dma = pltpu.SemaphoreType.DMA
    return pl.pallas_call(
        kernel,
        out_shape=jax.ShapeDtypeStruct((rows, width), BF16),
        in_specs=[smem, smem, anywhere, anywhere, vmem, vmem],
        out_specs=vmem,
        scratch_shapes=[
            pltpu.VMEM(blocks.shape, BF16),
            pltpu.VMEM((HALVES, 8, rows, half), BF16),
            pltpu.VMEM((HALVES, 33, 128, half), BF16),
            pltpu.VMEM((9, 128, 8), F32),
            pltpu.VMEM((16, 8, 128), F32),
            pltpu.VMEM((16, 8, 128), F32),
            pltpu.VMEM((8, 128), F32),
            pltpu.VMEM((8, 8, 128), F32),
            pltpu.VMEM((HALVES, 8, 2, rows, half), BF16),
            pltpu.VMEM((HALVES, 8, rows, half), BF16),
            pltpu.VMEM((HALVES, 8, rows, half), BF16),
            pltpu.VMEM((HALVES, 2, rows, half), BF16),
            pltpu.VMEM((HALVES, 2, rows, half), BF16),
            pltpu.VMEM((HALVES, 2, rows, half), BF16),
            pltpu.VMEM((HALVES, 4, rows, half), BF16),
            pltpu.VMEM((rows, width), BF16),
            dma((16,)), dma((HALVES,)), dma((128,)), dma((128,)),
        ],
        compiler_params=pltpu.CompilerParams(collective_id=0, has_side_effects=True, vmem_limit_bytes=58 << 20),
        cost_estimate=pl.CostEstimate(flops=4_300_000_000, bytes_accessed=17_000_000, transcendentals=1024),
    )(counts.T, block_cols.T, features, blocks, weight, bias.reshape(1, width))


def solution(mesh):
    return jax.shard_map(
        shards,
        mesh=mesh,
        in_specs=(
            P(("row", "col", "rep"), None),
            P("row", ("col", "rep"), None, None),
            P("row", ("col", "rep")),
            P("row", ("col", "rep")),
            P(),
            P(),
        ),
        out_specs=P(("row", "col", "rep"), None),
        check_vma=False,
    )
```

time: 294 us -> 67.5 us (0.23)
  waiting for transfers between devices: 121 us -> 0 us
  matrix products: 65.3 us -> 0 us
  Pallas kernels: 0 us -> 64.7 us
  blocking collectives: 56.7 us -> 0 us
  local copies, waits for them, and re-layouts: 24.9 us -> 1.67 us
  between operations: 14.2 us -> 0.01 us
  other arithmetic: 11.8 us -> 0 us
    reduce_scatter x1 -> x0, waiting for transfers between devices: 66.4 us -> none  [shards(): lax.psum_scatter(running.reshape(count, feature_width).astype(jnp.bfloat1...]
    dot_general x9 -> x0, matrix products: 65.3 us -> none  [the longest x8 63.4 us: shards(): jnp.einsum('iab,ibf->iaf', tile_values, picked, preferred_element_type=jn...]
    pallas_call x0 -> x1, Pallas kernels: none -> 64.7 us  [shards(): pl.pallas_call(kernel, out_shape=jax.ShapeDtypeStruct((rows, width), BF16...]
    unnamed x1 -> x0, blocking collectives: 56.7 us -> none
    all_gather x1 -> x0, waiting for transfers between devices: 54.3 us -> none  [shards(): gathered = lax.all_gather(scaled, 'row', axis=0, tiled=True)]
    gather x8 -> x0, local copies, waits for them, and re-layouts: 24.1 us -> none  [shards(): picked = jnp.take(panel_blocks, column_index, axis=0)]
    reduce_sum x2 -> x0, other arithmetic: 10.2 us -> none  [the longest x1 10 us: shards(): block_sums = jnp.sum(blocks, axis=3, dtype=jnp.float32)]
  transfers between devices with their start and end apart: 2 -> 0, of which waited for: 2 -> 0; matrix products, arithmetic and copies ran while one was open for 0% -> 0% of each run, Pallas kernels for 0% -> 0%
where the time goes in v1:
time: 67.5 us; the launch traced here: 66.4 us
  Pallas kernels  64.7 us (96%)
  local copies, waits for them, and re-layouts  1.67 us (2%)
    pallas_call x1, Pallas kernels, shards(): pl.pallas_call(kernel, out_shape=jax.ShapeDtypeStruct((rows, width), BF16...  64.7 us
    unnamed x1, local copies, waits for them, and re-layouts  1.67 us

profile of v1, /device:TPU:0, one launch (start us, length us, event | category | flops | bytes accessed | tf_op | source)
XLA Modules:
  0.0 66.4 jit_solution(536519118922059348)
XLA Ops:
  0.0 64.7 %shard_map.64 = bf16[512,256]{1,0:T(8,128)(2,1)} custom-call(s32[1,64]{1,0:T(1,128)} %bitcast.5, s32[8,64]{1,0:T(8,128)} %bitcast.3, bf16[512,256]{1,0:T(8,128)(2,1)} %feat.1, bf16[64,8,128,128]{3,2,1,0:T(8,128)(2,1)} %blocks.1, bf16[256,256]{1,0:T(8,128)(2,1)} %weight.1, f32[1,256]{1,0:T(1,128)} %bitcast.4), custom_call_target="tpu_custom_call" | custom-call | flops 4300000256 | bytes 17000000 | tf_op jit(solution)/shard_map/pallas_call | solution.py:310
  64.7 1.7 %copy.8 = bf16[512,256]{1,0:T(8,128)(2,1)} copy(bf16[512,256]{1,0:T(8,128)(2,1)} %shard_map.64) | data formatting | bytes 524288

commit v2 on v0

v2 whole, which is shorter than its diff:
```python
import contextlib
import math

import jax
import jax.numpy as jnp
from jax import lax
from jax.experimental import pallas as pl
from jax.experimental.pallas import tpu as pltpu
from jax.sharding import PartitionSpec as P

MESH = pl.DeviceIdType.MESH
BF16, F32 = jnp.bfloat16, jnp.float32
HALVES = 2
SCOPES = False
PRE = 3
GATHER_Z = 384
REDUCE_Z = (0, 0)
DEPTH = 6
FILL = 9
EARLY = 0
CHUNKS = ((2, 1, 0), (2, 1, 1), (2, 0, 0), (2, 0, 1), (1, 1, 0), (1, 1, 1), (3, 1, 0), (3, 1, 1), (1, 0, 0), (1, 0, 1), (3, 0, 0),
          (3, 0, 1), (0, 1, 0), (0, 1, 1), (0, 0, 1), (0, 0, 0))
N_SEM = 66 + 16 * (GATHER_Z < 512) + 8 * (REDUCE_Z[1] > 0)
UNITS = (((2, 0), (2, 1)), ((1, 0), (3, 0)), ((1, 1), (3, 1)), ((0, 0), (0, 1)))
FAR = ((2, 0, 0), (2, 0, 1), (2, 1, 0), (2, 1, 1))
NEAR = [((1, zc, 1), (3, zc, 0)) for zc in (0, 1)]
NEXT = [((1, zc, 0), (3, zc, 1)) for zc in (0, 1)]
HOME = [((0, zc, 0), (0, zc, 1)) for zc in (0, 1)]


def schedule():
    def close(h, *groups):
        return [("close", h, *which) for group in groups for which in group]

    steps = [("sums", k) for k in range(PRE)] + [("barrier",), ("g_own", 0, 0), ("g_far", 0), ("g_own", 0, 1)]
    steps += [("sums", k) for k in range(PRE, FILL)] + [("g_own", 1, 0)]
    steps += [("sums", k) for k in range(FILL, 16)]
    steps += [("g_relay", 0), ("g_z", 0), ("send_roots",), ("g_far", 1)] + [("g_relay", 1), ("g_own", 1, 1)] * EARLY
    steps += [("g_out", 0), ("g_zrelay", 0)] + [("g_relay", 1), ("g_own", 1, 1)] * (not EARLY)
    steps += [("inputs",), ("turn_roots",), ("scale", 0, 0), ("g_z", 1), ("g_rest", 0), ("scale", 0, 1)]
    steps += [("unit", 0, 0), ("g_out", 1), ("unit", 0, 1), *close(0, FAR), ("g_zrelay", 1), ("unit", 0, 2), *close(0, NEAR[0])]
    steps += [("unit", 0, 3), ("scale", 1, 0), *close(0, NEXT[0], NEAR[1], NEXT[1]), ("g_rest", 1), ("scale", 1, 1)]
    steps += [("unit", 1, 0), ("unit", 1, 1), *close(1, FAR[:2]), *close(0, HOME[0]), ("unit", 1, 2), *close(1, NEAR[0])]
    steps += [*close(1, FAR[2:]), ("unit", 1, 3), *close(1, NEXT[0], NEAR[1]), *close(0, HOME[1]), *close(1, NEXT[1], HOME[0])]
    steps += [("drain",), *close(1, HOME[1][:1]), ("output", 0), *close(1, HOME[1][1:]), ("output", 1), ("leave",)]
    return steps


def kernel(cnt_in, cols_in, feat, blocks, weight_in, bias_in, out, cnt, cols, weight, bias, o_v, blk, raw, pan, inv_t, rs_tx, rs_rx, inv_tx, inv_rx, part, sib_rx, acc,
           ab_rx, p_rx, m_rx, z_rx, agg, isem, osem, bsem, fsem, ssem, rsem):
    row, col, rep = lax.axis_index("row"), lax.axis_index("col"), lax.axis_index("rep")
    x, zh, zl, c = row // 2, row % 2, rep // 2, rep % 2
    q = col * 4 + rep
    n_chunk = 16
    brows = blk.shape[0] // n_chunk
    width = raw.shape[-1]

    def row_peer(i):
        return (lax.rem(row + i, 8), col, rep)

    def col_peer(i):
        p = lax.rem(q + i, 16)
        return (row, p // 4, p % 4)

    sib = (row, col, zl * 2 + 1 - c)
    y_next, y_prev = (row, lax.rem(col + 1, 4), rep), (row, lax.rem(col + 3, 4), rep)
    z_near = (row, col, (1 - zl) * 2 + c)
    x_next, x_prev = (lax.rem(x + 1, 4) * 2 + zh, col, rep), (lax.rem(x + 3, 4) * 2 + zh, col, rep)
    z_far = (x * 2 + 1 - zh, col, rep)

    def start(src, dst, sem):
        copy = pltpu.make_async_copy(src, dst, sem)
        copy.start()
        return copy

    feat_copies = [start(feat.at[:, pl.ds(h * width, width)], raw.at[h, row], fsem.at[h]) for h in range(HALVES)]
    cnt_copy = start(cnt_in, cnt, isem.at[0])

    block_copies = []

    def place_of(dy, dz, dc):
        return lax.rem(col + dy, 4), zl + dz - 2 * dz * zl, c + dc - 2 * dc * c

    def chunk_rows(k):
        y_, z_, c_ = place_of(*CHUNKS[k])
        return (y_ * 4 + z_ * 2 + c_) * brows

    def fetch(k):
        here = pl.ds(chunk_rows(k), brows)
        block_copies.append(start(blocks.at[here], blk.at[here], bsem.at[k % DEPTH]))

    barrier = pltpu.get_barrier_semaphore()
    fetch(0)
    for i in range(1, 8):
        pl.semaphore_signal(barrier, inc=1, device_id=row_peer(i), device_id_type=MESH)
    fetch(1)
    for i in range(1, 16):
        pl.semaphore_signal(barrier, inc=1, device_id=col_peer(i), device_id_type=MESH)
    for k in range(2, DEPTH):
        fetch(k)
    late_copies = [
        start(src, dst, isem.at[i + 1]) for i, (src, dst) in enumerate(((cols_in, cols), (weight_in, weight), (bias_in, bias)))
    ]

    numbers, pending = {}, [0, 0]

    def number(name):
        return numbers.setdefault(name, len(numbers))

    def send(name, src, dst, device, small=0):
        pltpu.make_async_remote_copy(
            src_ref=src, dst_ref=dst, send_sem=ssem.at[small], recv_sem=rsem.at[number(name)], device_id=device, device_id_type=MESH
        ).start()
        pending[small] += math.prod(src.shape) * src.dtype.itemsize

    def recv(name, place):
        pltpu.make_async_copy(place, place, rsem.at[number(name)]).wait()

    rs_tx[...] = jnp.zeros_like(rs_tx)
    for h in range(HALVES):
        pan[h, 32] = jnp.zeros((128, width), BF16)

    def row_sums(k):
        if k == 0:
            cnt_copy.wait()
        block_copies[k].wait()
        if k + DEPTH < n_chunk:
            fetch(k + DEPTH)
        first = chunk_rows(k)
        for j in range(brows):
            i = first + j
            live = cnt[0, i]
            total = jnp.zeros((128, 128), F32)
            for s in range(8):
                total = total + jnp.where(s < live, blk[i, s].astype(F32), 0.0)
            rs_tx[k, j : j + 1, :] = jnp.sum(total.T, axis=0, keepdims=True)
        if k >= PRE:
            send_sum(k)

    def send_sum(k):
        if k < n_chunk - 1:
            y_, z_, c_ = place_of(*CHUNKS[k])
            send("sums", rs_tx.at[k], rs_rx.at[q], (row, y_, z_ * 2 + c_), small=1)
        else:
            rs_rx[q] = rs_tx[k]

    half_z = GATHER_Z // 2
    mid = (pl.ds(256 - half_z, half_z), pl.ds(256, half_z))
    outer = (pl.ds(0, 256 - half_z), pl.ds(256 + half_z, 256 - half_z))
    side_rows = (pl.ds(0, 256), pl.ds(256, 256))
    at_next, at_prev, at_two = lax.rem(x + 1, 4), lax.rem(x + 3, 4), lax.rem(x + 2, 4)

    def piece(h, xs, z, rows):
        return raw.at[h, xs * 2 + z, rows]

    def copied(name, h, place, device):
        send((name, h), place, place, device)

    def outward(h, what, xs, side):
        if GATHER_Z < 512:
            copied(("out", what, side), h, piece(h, xs, zh, outer[side]), z_far)

    def gather_own(h, part):
        if part == 0:
            feat_copies[h].wait()
        copied(("own+", part), h, piece(h, x, zh, side_rows[part]), x_next)
        copied(("own-", 1 - part), h, piece(h, x, zh, side_rows[1 - part]), x_prev)

    def gather_far(h):
        for side in (0, 1):
            copied(("z", side), h, piece(h, x, zh, mid[side]), z_far)
        for side in (0, 1):
            outward(h, 0, x, side)

    def gather_relay(h):
        recv((("own+", 0), h), piece(h, at_prev, zh, side_rows[0]))
        copied("relay+", h, piece(h, at_prev, zh, side_rows[0]), x_next)
        recv((("own-", 1), h), piece(h, at_next, zh, side_rows[1]))
        copied("relay-", h, piece(h, at_next, zh, side_rows[1]), x_prev)
        outward(h, 1, at_prev, 0)
        outward(h, 2, at_next, 1)

    def gather_z(h):
        for side in (0, 1):
            place = piece(h, x, 1 - zh, mid[side])
            recv((("z", side), h), place)
            copied(("z+", side), h, place, x_next)
            copied(("z-", side), h, place, x_prev)

    def gather_out(h):
        recv((("own+", 1), h), piece(h, at_prev, zh, side_rows[1]))
        outward(h, 1, at_prev, 1)
        recv((("own-", 0), h), piece(h, at_next, zh, side_rows[0]))
        outward(h, 2, at_next, 0)

    def gather_zrelay(h):
        place = piece(h, at_prev, 1 - zh, mid[0])
        recv((("z+", 0), h), place)
        copied("zrelay+", h, place, x_next)
        place = piece(h, at_next, 1 - zh, mid[1])
        recv((("z-", 1), h), place)
        copied("zrelay-", h, place, x_prev)
        recv(("relay+", h), piece(h, at_two, zh, side_rows[0]))
        outward(h, 3, at_two, 0)
        recv(("relay-", h), piece(h, at_two, zh, side_rows[1]))
        outward(h, 3, at_two, 1)

    def gather_rest(h):
        recv((("z+", 1), h), piece(h, at_prev, 1 - zh, mid[1]))
        recv((("z-", 0), h), piece(h, at_next, 1 - zh, mid[0]))
        recv(("zrelay+", h), piece(h, at_two, 1 - zh, mid[0]))
        recv(("zrelay-", h), piece(h, at_two, 1 - zh, mid[1]))
        if GATHER_Z < 512:
            for what, xs in enumerate((x, at_prev, at_next, at_two)):
                for side in (0, 1):
                    recv((("out", what, side), h), piece(h, xs, 1 - zh, outer[side]))

    def scale(h, part):
        def group(xs, z):
            r = xs * 2 + z
            for j in range(4):
                rows = pl.ds(j * 128, 128)
                factor = inv_t[r, :, j : j + 1]
                pan[h, r * 4 + j] = (raw[h, r, rows, :].astype(F32) * factor).astype(BF16)

        if part == 0:
            for xs in (x, at_prev, at_next, at_two):
                group(xs, zh)
        else:
            for xs in (x, at_prev, at_next, at_two):
                group(xs, 1 - zh)

    def product(halves, slot, side, chip, core):
        first = (chip * 2 + core) * 4
        for j in range(4):
            i = first + j
            live = cnt[0, i]
            at = [jnp.where(s < live, cols[s, i], 32) for s in range(8)]
            picked = jnp.concatenate(
                [jnp.concatenate([pan[h, at[s]] for s in range(8)], axis=0) for h in halves], axis=1
            )
            tile = jnp.concatenate([blk[i, s] for s in range(8)], axis=1)
            total = jnp.dot(tile, picked, preferred_element_type=F32).astype(BF16)
            for n, h in enumerate(halves):
                part[h, side, slot, pl.ds(j * 128, 128), :] = total[:, n * width : (n + 1) * width]

    def unit(h, number):
        pairs = UNITS[number]
        for side, core in ((0, 1 - c), (1, c)):
            for n, (off, zc) in enumerate(pairs):
                chip = lax.rem(col + off, 4) * 2 + (zl if zc else 1 - zl)
                product((h,), number * 2 + n, side, chip, core)
        here = pl.ds(number * 2, 2)
        send(("sib", h, number), part.at[h, 0, here], sib_rx.at[h, here], sib)

    at_home = set()

    def moved(name, src, dst, device, lo, hi):
        if hi > lo:
            rows = pl.ds(lo, hi - lo)
            send(name, src.at[rows], dst.at[rows], device)

    def arrived(name, dst, lo, hi):
        if hi > lo:
            recv(name, dst.at[pl.ds(lo, hi - lo)])

    def close(h, off, zc, side):
        number, n = next((u, p.index((off, zc))) for u, p in enumerate(UNITS) if (off, zc) in p)
        slot = number * 2 + n
        last = zc == 1 and off == 0
        if (h, number) not in at_home:
            at_home.add((h, number))
            recv(("sib", h, number), sib_rx.at[h, pl.ds(number * 2, 2)])
        ra, rb = 256 - REDUCE_Z[h] // 2, 256 + REDUCE_Z[h] // 2
        outer_r, mid_r = ((0, ra), (ra, 256)) if side == 0 else ((rb, 512), (256, rb))
        lo, hi = (side * 256, side * 256 + 256) if zc else outer_r
        takes_ab = (off, side) in ((1, 0), (3, 1))
        if takes_ab:
            arrived(("ab", h, zc, side), ab_rx.at[h, zc], lo, hi)
        if off == 0:
            arrived(("p", h, zc, side), p_rx.at[h, zc], lo, hi)
            arrived(("m", h, zc, side), m_rx.at[h, zc], lo, hi)
        if zc == 1:
            arrived(("zm", h, off, side), z_rx.at[h, off], *mid_r)
            if off == 0:
                arrived(("zo", h, off, side), z_rx.at[h, off], *outer_r)
        for is_mid, (a, b) in enumerate((outer_r, mid_r)):
            if b == a:
                continue
            rows = pl.ds(a, b - a)
            round_y = zc == 1 or not is_mid
            total = part[h, 1, slot, rows, :].astype(F32) + sib_rx[h, slot, rows, :].astype(F32)
            if takes_ab and round_y:
                total = total + ab_rx[h, zc, rows, :].astype(F32)
            if off == 0 and round_y:
                total = total + p_rx[h, zc, rows, :].astype(F32) + m_rx[h, zc, rows, :].astype(F32)
            if zc == 1 and (is_mid or off == 0):
                total = total + z_rx[h, off, rows, :].astype(F32)
            if last:
                finish(h, a, b, total)
            else:
                acc[h, slot, rows, :] = total.astype(BF16)
        src = acc.at[h, slot]
        if zc == 0:
            moved(("zm", h, off, side), src, z_rx.at[h, off], z_near, *mid_r)
            if off == 0:
                moved(("zo", h, off, side), src, z_rx.at[h, off], z_near, *outer_r)
        if off == 2:
            moved(("ab", h, zc, side), src, ab_rx.at[h, zc], y_prev if side else y_next, lo, hi)
        if off == 1:
            moved(("p", h, zc, side), src, p_rx.at[h, zc], y_next, lo, hi)
        if off == 3:
            moved(("m", h, zc, side), src, m_rx.at[h, zc], y_prev, lo, hi)

    def finish(h, a, b, total):
        while a < b:
            j, end = a // 128, min(b, a // 128 * 128 + 128)
            factor = inv_t[8, a - j * 128 : end - j * 128, j : j + 1]
            own = pan[h, row * 4 + j, a - j * 128 : end - j * 128, :].astype(F32)
            agg[a:end, h * width : (h + 1) * width] = (factor * (total[: end - a] + own)).astype(BF16)
            total, a = total[end - a :], end

    def output(side):
        for j in (side * 2, side * 2 + 1):
            rows = pl.ds(j * 128, 128)
            mixed = jnp.dot(agg[rows, :], weight[...], preferred_element_type=F32) + bias[...]
            o_v[rows, :] = jnp.maximum(mixed, 0.0).astype(BF16)
            out_copies.append(start(o_v.at[rows], out.at[rows], osem.at[j]))

    out_copies = []

    def leave():
        for copy in out_copies:
            copy.wait()

    def drain():
        for n, (ref, unit_bytes) in enumerate(((blk, blk.shape[1] * 128 * 256), (o_v, o_v.shape[1] * 2))):
            assert pending[n] % unit_bytes == 0
            here = ref.at[pl.ds(0, pending[n] // unit_bytes)]
            pltpu.make_async_copy(here, here, ssem.at[n]).wait()

    def inputs():
        for copy in late_copies:
            copy.wait()

    def send_roots():
        recv("sums", rs_rx.at[pl.ds(0, 15)])
        degree = rs_rx[0]
        for i in range(1, 16):
            degree = degree + rs_rx[i]
        inv_tx[...] = lax.rsqrt(1.0 + degree)
        for i in range(1, 8):
            send("roots", inv_tx, inv_rx.at[row], row_peer(i), small=1)
        inv_rx[row] = inv_tx[...]

    def turn_roots():
        recv("roots", inv_rx.at[pl.ds(0, 7)])
        for r in range(8):
            inv_t[r] = inv_rx[r].T
        inv_t[8] = inv_tx[...].T

    def pass_barrier():
        pl.semaphore_wait(barrier, 22)
        for k in range(PRE):
            send_sum(k)

    work = {
        "sums": row_sums, "barrier": pass_barrier, "g_own": gather_own, "g_relay": gather_relay, "g_far": gather_far, "g_z": gather_z, "g_out": gather_out,
        "g_zrelay": gather_zrelay, "g_rest": gather_rest, "send_roots": send_roots,
        "turn_roots": turn_roots, "scale": scale, "unit": unit, "close": close, "output": output, "leave": leave,
        "drain": drain, "inputs": inputs,
    }
    for name, *args in schedule():
        with jax.named_scope("_".join(map(str, (name, *args)))) if SCOPES else contextlib.nullcontext():
            work[name](*args)
    assert len(numbers) == N_SEM, len(numbers)


def shards(features, blocks, block_cols, counts, weight, bias):
    rows, width = features.shape
    half = width // HALVES
    anywhere = pl.BlockSpec(memory_space=pl.ANY)
    dma = pltpu.SemaphoreType.DMA
    return pl.pallas_call(
        kernel,
        out_shape=jax.ShapeDtypeStruct((rows, width), BF16),
        in_specs=[anywhere] * 6,
        out_specs=anywhere,
        scratch_shapes=[
            pltpu.SMEM((1, blocks.shape[0]), jnp.int32),
            pltpu.SMEM((8, blocks.shape[0]), jnp.int32),
            pltpu.VMEM((width, width), BF16),
            pltpu.VMEM((1, width), F32),
            pltpu.VMEM((rows, width), BF16),
            pltpu.VMEM(blocks.shape, BF16),
            pltpu.VMEM((HALVES, 8, rows, half), BF16),
            pltpu.VMEM((HALVES, 33, 128, half), BF16),
            pltpu.VMEM((9, 128, 8), F32),
            pltpu.VMEM((16, 8, 128), F32),
            pltpu.VMEM((16, 8, 128), F32),
            pltpu.VMEM((8, 128), F32),
            pltpu.VMEM((8, 8, 128), F32),
            pltpu.VMEM((HALVES, 2, 8, rows, half), BF16),
            pltpu.VMEM((HALVES, 8, rows, half), BF16),
            pltpu.VMEM((HALVES, 8, rows, half), BF16),
            pltpu.VMEM((HALVES, 2, rows, half), BF16),
            pltpu.VMEM((HALVES, 2, rows, half), BF16),
            pltpu.VMEM((HALVES, 2, rows, half), BF16),
            pltpu.VMEM((HALVES, 4, rows, half), BF16),
            pltpu.VMEM((rows, width), BF16),
            dma((4,)), dma((4,)), dma((DEPTH,)), dma((HALVES,)), dma((2,)), dma((N_SEM,)),
        ],
        compiler_params=pltpu.CompilerParams(collective_id=0, has_side_effects=True, vmem_limit_bytes=58 << 20),
        cost_estimate=pl.CostEstimate(flops=4_300_000_000, bytes_accessed=17_000_000, transcendentals=1024),
    )(counts.T, block_cols.T, features, blocks, weight, bias.reshape(1, width))


def solution(mesh):
    return jax.shard_map(
        shards,
        mesh=mesh,
        in_specs=(
            P(("row", "col", "rep"), None),
            P("row", ("col", "rep"), None, None),
            P("row", ("col", "rep")),
            P("row", ("col", "rep")),
            P(),
            P(),
        ),
        out_specs=P(("row", "col", "rep"), None),
        check_vma=False,
    )
```

time: 294 us -> 48.8 us (0.17)
  waiting for transfers between devices: 121 us -> 0 us
  matrix products: 65.3 us -> 0 us
  blocking collectives: 56.7 us -> 0 us
  Pallas kernels: 0 us -> 47 us
  local copies, waits for them, and re-layouts: 24.9 us -> 1.67 us
  between operations: 14.2 us -> 0.01 us
  other arithmetic: 11.8 us -> 0 us
    reduce_scatter x1 -> x0, waiting for transfers between devices: 66.4 us -> none  [shards(): lax.psum_scatter(running.reshape(count, feature_width).astype(jnp.bfloat1...]
    dot_general x9 -> x0, matrix products: 65.3 us -> none  [the longest x8 63.4 us: shards(): jnp.einsum('iab,ibf->iaf', tile_values, picked, preferred_element_type=jn...]
    unnamed x1 -> x0, blocking collectives: 56.7 us -> none
    all_gather x1 -> x0, waiting for transfers between devices: 54.3 us -> none  [shards(): gathered = lax.all_gather(scaled, 'row', axis=0, tiled=True)]
    pallas_call x0 -> x1, Pallas kernels: none -> 47 us  [shards(): pl.pallas_call(kernel, out_shape=jax.ShapeDtypeStruct((rows, width), BF16...]
    gather x8 -> x0, local copies, waits for them, and re-layouts: 24.1 us -> none  [shards(): picked = jnp.take(panel_blocks, column_index, axis=0)]
    reduce_sum x2 -> x0, other arithmetic: 10.2 us -> none  [the longest x1 10 us: shards(): block_sums = jnp.sum(blocks, axis=3, dtype=jnp.float32)]
  transfers between devices with their start and end apart: 2 -> 0, of which waited for: 2 -> 0; matrix products, arithmetic and copies ran while one was open for 0% -> 0% of each run, Pallas kernels for 0% -> 0%
where the time goes in v2:
time: 48.8 us; the launch traced here: 48.7 us
  Pallas kernels  47 us (96%)
  local copies, waits for them, and re-layouts  1.67 us (3%)
    pallas_call x1, Pallas kernels, shards(): pl.pallas_call(kernel, out_shape=jax.ShapeDtypeStruct((rows, width), BF16...  47 us
    unnamed x1, local copies, waits for them, and re-layouts  1.67 us

profile of v2, /device:TPU:0, one launch (start us, length us, event | category | flops | bytes accessed | tf_op | source)
XLA Modules:
  0.0 48.7 jit_solution(17173064421635207032)
XLA Ops:
  0.0 47.0 %shard_map.64 = bf16[512,256]{1,0:T(8,128)(2,1)} custom-call(s32[1,64]{1,0:T(1,128)} %bitcast.5, s32[8,64]{1,0:T(8,128)} %bitcast.3, bf16[512,256]{1,0:T(8,128)(2,1)} %feat.1, bf16[64,8,128,128]{3,2,1,0:T(8,128)(2,1)} %blocks.1, bf16[256,256]{1,0:T(8,128)(2,1)} %weight_in.1, f32[1,256]{1,0:T(1,128)} %bitcast.4), custom_call_target="tpu_custom_call" | custom-call | flops 4300000256 | bytes 17000000 | tf_op jit(solution)/shard_map/pallas_call | solution.py:384
  47.0 1.7 %copy.8 = bf16[512,256]{1,0:T(8,128)(2,1)} copy(bf16[512,256]{1,0:T(8,128)(2,1)} %shard_map.64) | data formatting | bytes 524288

commit v3 on v2

--- a/solution.py
+++ b/solution.py
@@ -14,13 +14,14 @@
 SCOPES = False
 PRE = 3
 GATHER_Z = 384
-REDUCE_Z = (0, 0)
+STALL = 0
+FAR_SOON = 1
+REDUCE_Z = (0, 128)
 DEPTH = 6
 FILL = 9
-EARLY = 0
-CHUNKS = ((2, 1, 0), (2, 1, 1), (2, 0, 0), (2, 0, 1), (1, 1, 0), (1, 1, 1), (3, 1, 0), (3, 1, 1), (1, 0, 0), (1, 0, 1), (3, 0, 0),
-          (3, 0, 1), (0, 1, 0), (0, 1, 1), (0, 0, 1), (0, 0, 0))
-N_SEM = 66 + 16 * (GATHER_Z < 512) + 8 * (REDUCE_Z[1] > 0)
+CHUNKS = tuple((dy, dz, dc) for dz in (1, 0) for dy in (2, 1, 3, 0) for dc in (0, 1))
+CHUNKS = CHUNKS[:-2] + CHUNKS[:-3:-1]
+N_SEM = 66 + 16 * (GATHER_Z < 512) + 8 * sum(z > 0 for z in REDUCE_Z)
 UNITS = (((2, 0), (2, 1)), ((1, 0), (3, 0)), ((1, 1), (3, 1)), ((0, 0), (0, 1)))
 FAR = ((2, 0, 0), (2, 0, 1), (2, 1, 0), (2, 1, 1))
 NEAR = [((1, zc, 1), (3, zc, 0)) for zc in (0, 1)]
@@ -35,13 +36,16 @@
     steps = [("sums", k) for k in range(PRE)] + [("barrier",), ("g_own", 0, 0), ("g_far", 0), ("g_own", 0, 1)]
     steps += [("sums", k) for k in range(PRE, FILL)] + [("g_own", 1, 0)]
     steps += [("sums", k) for k in range(FILL, 16)]
-    steps += [("g_relay", 0), ("g_z", 0), ("send_roots",), ("g_far", 1)] + [("g_relay", 1), ("g_own", 1, 1)] * EARLY
-    steps += [("g_out", 0), ("g_zrelay", 0)] + [("g_relay", 1), ("g_own", 1, 1)] * (not EARLY)
-    steps += [("inputs",), ("turn_roots",), ("scale", 0, 0), ("g_z", 1), ("g_rest", 0), ("scale", 0, 1)]
-    steps += [("unit", 0, 0), ("g_out", 1), ("unit", 0, 1), *close(0, FAR), ("g_zrelay", 1), ("unit", 0, 2), *close(0, NEAR[0])]
-    steps += [("unit", 0, 3), ("scale", 1, 0), *close(0, NEXT[0], NEAR[1], NEXT[1]), ("g_rest", 1), ("scale", 1, 1)]
-    steps += [("unit", 1, 0), ("unit", 1, 1), *close(1, FAR[:2]), *close(0, HOME[0]), ("unit", 1, 2), *close(1, NEAR[0])]
-    steps += [*close(1, FAR[2:]), ("unit", 1, 3), *close(1, NEXT[0], NEAR[1]), *close(0, HOME[1]), *close(1, NEXT[1], HOME[0])]
+    steps += [("g_relay", 0), ("g_z", 0, 0), ("send_roots",), ("g_z", 0, 1)] + [("g_far", 1)] * FAR_SOON
+    steps += [("g_out", 0), ("g_zrelay", 0)] + [("g_far", 1)] * (not FAR_SOON) + [("g_relay", 1), ("g_own", 1, 1)]
+    steps += [("inputs",), ("turn_roots",), ("scale", 0, 0), ("g_z", 1, 0), ("g_z", 1, 1), ("g_rest", 0), ("scale", 0, 1)]
+    soon = 2 if REDUCE_Z[0] else 4
+    steps += [("unit", 0, 0), ("g_out", 1), ("unit", 0, 1), *close(0, FAR[:soon]), ("g_zrelay", 1)]
+    steps += [("unit", 0, 2), *close(0, FAR[soon:], NEAR[0]), ("unit", 0, 3), *close(0, NEAR[1]), ("scale", 1, 0)]
+    steps += [*close(0, NEXT[0]) * (not STALL), ("g_rest", 1), ("scale", 1, 1), ("unit", 1, 0), *close(0, NEXT[0]) * STALL]
+    steps += [("unit", 1, 1), *close(0, NEXT[1]), *close(1, FAR[:2]), ("unit", 1, 2), *close(1, NEAR[0])]
+    steps += [("unit", 1, 3), *close(1, FAR[2:]), *close(0, HOME[0]), *close(1, NEXT[0], NEAR[1], NEXT[1], HOME[0])]
+    steps += [*close(0, HOME[1])]
     steps += [("drain",), *close(1, HOME[1][:1]), ("output", 0), *close(1, HOME[1][1:]), ("output", 1), ("leave",)]
     return steps
 
@@ -180,12 +184,12 @@
         outward(h, 1, at_prev, 0)
         outward(h, 2, at_next, 1)
 
-    def gather_z(h):
-        for side in (0, 1):
-            place = piece(h, x, 1 - zh, mid[side])
-            recv((("z", side), h), place)
-            copied(("z+", side), h, place, x_next)
-            copied(("z-", side), h, place, x_prev)
+    def gather_z(h, part):
+        if part == 0:
+            for side in (0, 1):
+                recv((("z", side), h), piece(h, x, 1 - zh, mid[side]))
+        copied(("z+", part), h, piece(h, x, 1 - zh, mid[part]), x_next)
+        copied(("z-", 1 - part), h, piece(h, x, 1 - zh, mid[1 - part]), x_prev)
 
     def gather_out(h):
         recv((("own+", 1), h), piece(h, at_prev, zh, side_rows[1]))

time: 48.8 us -> 47.5 us (0.973)
  Pallas kernels: 47 us -> 45.7 us
    pallas_call x1, Pallas kernels: 47 us -> 45.7 us  [shards(): pl.pallas_call(kernel, out_shape=jax.ShapeDtypeStruct((rows, width), BF16...]
where the time goes in v3:
time: 47.5 us; the launch traced here: 47.4 us
  Pallas kernels  45.7 us (96%)
  local copies, waits for them, and re-layouts  1.67 us (4%)
    pallas_call x1, Pallas kernels, shards(): pl.pallas_call(kernel, out_shape=jax.ShapeDtypeStruct((rows, width), BF16...  45.7 us
    unnamed x1, local copies, waits for them, and re-layouts  1.67 us

profile of v3, /device:TPU:0, one launch (start us, length us, event | category | flops | bytes accessed | tf_op | source)
XLA Modules:
  0.0 47.4 jit_solution(13905237912336275003)
XLA Ops:
  0.0 45.7 %shard_map.64 = bf16[512,256]{1,0:T(8,128)(2,1)} custom-call(s32[1,64]{1,0:T(1,128)} %bitcast.5, s32[8,64]{1,0:T(8,128)} %bitcast.3, bf16[512,256]{1,0:T(8,128)(2,1)} %feat.1, bf16[64,8,128,128]{3,2,1,0:T(8,128)(2,1)} %blocks.1, bf16[256,256]{1,0:T(8,128)(2,1)} %weight_in.1, f32[1,256]{1,0:T(1,128)} %bitcast.4), custom_call_target="tpu_custom_call" | custom-call | flops 4300000256 | bytes 17000000 | tf_op jit(solution)/shard_map/pallas_call | solution.py:388
  45.7 1.7 %copy.8 = bf16[512,256]{1,0:T(8,128)(2,1)} copy(bf16[512,256]{1,0:T(8,128)(2,1)} %shard_map.64) | data formatting | bytes 524288

commit v4 on v3

--- a/solution.py
+++ b/solution.py
@@ -16,7 +16,7 @@
 GATHER_Z = 384
 STALL = 0
 FAR_SOON = 1
-REDUCE_Z = (0, 128)
+REDUCE_Z = (0, 192)
 DEPTH = 6
 FILL = 9
 CHUNKS = tuple((dy, dz, dc) for dz in (1, 0) for dy in (2, 1, 3, 0) for dc in (0, 1))

time: 47.5 us -> 48 us (1.011)
  Pallas kernels: 45.7 us -> 46.2 us
    pallas_call x1, Pallas kernels: 45.7 us -> 46.2 us  [shards(): pl.pallas_call(kernel, out_shape=jax.ShapeDtypeStruct((rows, width), BF16...]
where the time goes in v4:
time: 48 us; the launch traced here: 47.9 us
  Pallas kernels  46.2 us (96%)
  local copies, waits for them, and re-layouts  1.67 us (3%)
    pallas_call x1, Pallas kernels, shards(): pl.pallas_call(kernel, out_shape=jax.ShapeDtypeStruct((rows, width), BF16...  46.2 us
    unnamed x1, local copies, waits for them, and re-layouts  1.67 us

profile of v4, /device:TPU:0, one launch (start us, length us, event | category | flops | bytes accessed | tf_op | source)
XLA Modules:
  0.0 47.9 jit_solution(6868753729420916956)
XLA Ops:
  0.0 46.2 %shard_map.64 = bf16[512,256]{1,0:T(8,128)(2,1)} custom-call(s32[1,64]{1,0:T(1,128)} %bitcast.5, s32[8,64]{1,0:T(8,128)} %bitcast.3, bf16[512,256]{1,0:T(8,128)(2,1)} %feat.1, bf16[64,8,128,128]{3,2,1,0:T(8,128)(2,1)} %blocks.1, bf16[256,256]{1,0:T(8,128)(2,1)} %weight_in.1, f32[1,256]{1,0:T(1,128)} %bitcast.4), custom_call_target="tpu_custom_call" | custom-call | flops 4300000256 | bytes 17000000 | tf_op jit(solution)/shard_map/pallas_call | solution.py:388
  46.2 1.7 %copy.8 = bf16[512,256]{1,0:T(8,128)(2,1)} copy(bf16[512,256]{1,0:T(8,128)(2,1)} %shard_map.64) | data formatting | bytes 524288
